TPU v7x, 256 devices: a whole 4x4x8 slice. The times are simulated.
256 devices in a mesh: row: 32 (over y, x, core), col: 8 (over z).
Axes of the slice: x: 4, y: 4, z: 8, core: 2. Of those that a mesh axis runs over, the one named last changes fastest.
Arguments:
- hidden_slab: float32 [65536, 8192], P('row', 'col'), may hold values from -36 to 36, as said below
- test_matrix: float32 [8192, 288], P('col'), may hold values from -0.0625 to 0.0625
Outputs:
- basis_scaled: float32 [65536, 288], P('row')
- projected: float32 [288, 8192], P('row', 'col')
Inputs may be any that keep to these rules, and one draw needn't show every extreme that they name: hidden_slab holds real values with rows and columns of different scales.
All inputs are finite; a program needn't handle non-finite values.
Results may differ from a plain program's by a relative error of at most 0.0003.
Values sent between devices are 32-bit elements; how exact they have to be, the bound alone decides.
A program may use at most 64 MiB of HBM per device.

v0:
```python
import jax
import jax.numpy as jnp
from jax import lax
from jax.sharding import PartitionSpec as P


def on_device(hidden_slab, test_matrix):
    local_rows = hidden_slab.shape[0]
    total_rows = local_rows * lax.axis_size("row")
    partial_value = jnp.dot(
        hidden_slab,
        test_matrix,
        precision=lax.Precision.HIGHEST,
        preferred_element_type=jnp.float32,
    )
    sketch = lax.psum(partial_value, "col")
    gram_local = jnp.dot(
        sketch.T, sketch, precision=lax.Precision.HIGHEST, preferred_element_type=jnp.float32
    )
    gram = lax.psum(gram_local, "row")
    factor = jnp.linalg.cholesky(gram)
    basis = jax.scipy.linalg.solve_triangular(factor, sketch.T, lower=True).T
    projected = lax.psum_scatter(
        jnp.dot(
            basis.T,
            hidden_slab,
            precision=lax.Precision.HIGHEST,
            preferred_element_type=jnp.float32,
        ),
        "row",
        scatter_dimension=0,
        tiled=True,
    )
    return (basis * jnp.sqrt(jnp.float32(total_rows)), projected)


def solution(mesh):
    return jax.shard_map(
        on_device,
        mesh=mesh,
        in_specs=(P("row", "col"), P("col", None)),
        out_specs=(P("row", None), P("row", "col")),
        check_vma=False,
    )
```

profile of v0, /device:TPU:1, one launch (start us, length us, event | category | flops | bytes accessed | tf_op | source)
XLA Modules:
  0.0 486.9 jit_solution(1103471321999072324)
XLA Ops:
  8.4 11.5 %fusion.22 = f32[2048,288]{0,1:T(8,128)} fusion(f32[2048,1024]{1,0:T(8,128)} %param.2, f32[1024,288]{0,1:T(8,128)S(1)} %copy-done), kind=kOutput, calls=%fused_computation.58 | convolution fusion | flops 7247757312 | bytes 11927552 | tf_op jit(solution)/shard_map/dot_general | solution.py:10
  20.0 84.5 %all-reduce.8.cloned.1.call-done = f32[2048,288]{0,1:T(8,128)} async-done(((f32[2048,288]{0,1:T(8,128)}), f32[2048,288]{0,1:T(8,128)}) %all-reduce.8.cloned.1.call-update) | async-done | bytes 2359312 | tf_op jit(solution)/shard_map/psum | solution.py:16
  104.5 6.9 %fusion.23 = f32[288,288]{0,1:T(8,128)} fusion(f32[2048,288]{0,1:T(8,128)} %all-reduce.8.cloned.1.call-done), kind=kOutput, calls=%fused_computation.59 | convolution fusion | flops 2038431744 | bytes 2691072 | tf_op jit(solution)/shard_map/dot_general | solution.py:17
  112.9 113.3 %all-reduce.10.cloned.1.call-done = f32[288,288]{0,1:T(8,128)} async-done(((f32[288,288]{0,1:T(8,128)}), f32[288,288]{0,1:T(8,128)}) %all-reduce.10.cloned.1.call-update) | async-done | bytes 331792 | tf_op jit(solution)/shard_map/psum | solution.py:20
  229.9 13.3 %cholesky.78 = f32[128,128]{1,0:T(8,128)} custom-call(f32[128,128]{1,0:T(8,128)} %cholesky.198), custom_call_target="Cholesky" | custom-call | tf_op jit(solution)/shard_map/jit(cholesky)/cholesky | solution.py:21
  243.2 2.0 select_reduce_fusion.1
  245.2 11.3 %custom-call.23 = f32[1,128,128]{1,2,0:T(8,128)} custom-call(f32[1,128,128]{2,1,0:T(8,128)} %get-tuple-element.24), custom_call_target="InvertDiagBlocksLowerTriangular" | custom-call | tf_op jit(solution)/shard_map/jit(cholesky)/cholesky | solution.py:21
  258.1 1.7 constant_dynamic-update-slice_fusion.2
  262.2 13.2 %cholesky.164 = f32[128,128]{1,0:T(8,128)} custom-call(f32[128,128]{1,0:T(8,128)} %cholesky.202), custom_call_target="Cholesky" | custom-call | tf_op jit(solution)/shard_map/jit(cholesky)/cholesky | solution.py:21
  275.4 2.0 select_reduce_fusion
  277.4 11.5 %custom-call.24 = f32[1,128,128]{1,2,0:T(8,128)} custom-call(f32[1,128,128]{2,1,0:T(8,128)} %get-tuple-element.21), custom_call_target="InvertDiagBlocksLowerTriangular" | custom-call | tf_op jit(solution)/shard_map/jit(cholesky)/cholesky | solution.py:21
  288.9 1.6 convolution_dynamic-update-slice_fusion
  292.1 3.6 cholesky.186
  302.6 8.2 %while.1 = (s32[]{:T(128)}, f32[288,288]{1,0:T(8,128)}, s32[2,2]{1,0:T(2,128)}, f32[2,128,128]{2,1,0:T(8,128)}, s32[]{:T(128)}) while((s32[]{:T(128)}, f32[288,288]{1,0:T(8,128)}, s32[2,2]{1,0:T(2,128)}, f32[2,128,128]{2,1,0:T(8,128)}, s32[]{:T(128)}) %tuple.38), condition=%wide.while_cond, body=%wide.while_body.sunk | while | flops 2 | bytes 132705 | solution.py:22
  303.9 2.8 bitcast_dynamic-update-slice_fusion.2
  308.0 2.8 bitcast_dynamic-update-slice_fusion.2
  313.3 30.9 %custom-call.25 = f32[3,128,128]{1,2,0:T(8,128)} custom-call(f32[3,128,128]{2,1,0:T(8,128)} %pad_maximum_fusion.2), custom_call_target="InvertDiagBlocksLowerTriangular" | custom-call | tf_op jit(solution)/shard_map/jit(_solve_triangular)/triangular_solve | solution.py:22
  344.2 1.9 fusion.4
  346.1 1.9 convolution_subtract_fusion
  348.1 1.9 fusion.10
  350.0 2.1 convolution_subtract_fusion.1
  353.3 11.3 %fusion.3 = f32[288,1024]{1,0:T(8,128)} fusion(f32[2048,1024]{1,0:T(8,128)} %param.2, f32[32,2048]{1,0:T(8,128)S(1)} %fusion.17, f32[128,2048]{1,0:T(8,128)S(1)} %fusion.10, f32[128,2048]{1,0:T(8,128)S(1)} %fusion.4), kind=kOutput, calls=%fused_computation.9 | convolution fusion | flops 7248936960 | bytes 11927552 | tf_op jit(solution)/shard_map/dot_general | solution.py:24
  365.8 3.2 multiply_bitcast_fusion
  369.0 109.8 %all-reduce.12.cloned.1.call-done = f32[288,1024]{1,0:T(8,128)} async-done(((f32[288,1024]{1,0:T(8,128)}), f32[288,1024]{1,0:T(8,128)}) %all-reduce.12.cloned.1.call-update) | async-done | bytes 1179664
  (48 shorter events, 25.3 us)
Async XLA Ops:
  7.2 1.3 copy-start
  7.2 97.4 %all-reduce.8.cloned.1.call-start = ((), (), s32[]{:S(2)}) async-start(), calls=%async_computation | async-start | bytes 4718592 | tf_op jit(solution)/shard_map/psum | solution.py:16
  20.0 206.2 %all-reduce.10.cloned.1.call-start = ((), (), s32[]{:S(2)}) async-start(), calls=%async_computation.1 | async-start | bytes 884736 | tf_op jit(solution)/shard_map/psum | solution.py:20
  111.5 367.3 %all-reduce.12.cloned.1.call-start = ((), (), s32[]{:S(2)}) async-start(), calls=%async_computation.2 | async-start | bytes 2359296
  228.5 0.8 copy-start.5
  229.3 115.0 %copy-start.1 = (f32[2048,288]{0,1:T(8,128)S(1)}, f32[2048,288]{0,1:T(8,128)}, u32[]{:S(2)}) copy-start(f32[2048,288]{0,1:T(8,128)} %all-reduce.8.cloned.1.call-done) | copy-start | bytes 7077892
  261.0 0.6 copy-start.6
  301.3 1.3 copy-start.4
  346.1 7.1 %copy-start.2 = (f32[128,2048]{1,0:T(8,128)}, f32[128,2048]{1,0:T(8,128)S(1)}, u32[]{:S(2)}) copy-start(f32[128,2048]{1,0:T(8,128)S(1)} %fusion.4) | copy-start | bytes 3145732
  350.0 3.3 copy-start.3
  353.2 11.3 %copy-start.7 = (u32[256]{0:T(256)S(1)}, u32[256]{0:T(256)}, u32[]{:S(2)}) copy-start(u32[256]{0:T(256)} %constant.144) | copy-start | bytes 3076
Sparse Core Ops, SparseCore 0:
  20.1 84.4 all-reduce.7
  111.6 114.5 all-reduce.9
  364.7 114.1 all-reduce.11
where the time goes:
time: 488 us; the launch traced here: 487 us
  waiting for transfers between devices  308 us (63%)
  other arithmetic  99.3 us (20%)
  matrix products  44.8 us (9%)
  local copies, waits for them, and re-layouts  18.3 us (4%)
  between operations  16.5 us (3%)
    psum x1, waiting for transfers between devices, on_device(): gram = lax.psum(gram_local, 'row')  113 us
    unnamed x4, waiting for transfers between devices  110 us
    psum x1, waiting for transfers between devices, on_device(): sketch = lax.psum(partial_value, 'col')  84.5 us
    another operation x10, other arithmetic, on_device(): factor = jnp.linalg.cholesky(gram)  59.4 us
    another operation x7, other arithmetic, on_device(): basis = jax.scipy.linalg.solve_triangular(factor, sketch.T, lower=True).T  35.6 us
    dot_general x1, matrix products, on_device(): jnp.dot(hidden_slab, test_matrix, precision=lax.Precision.HIGHEST, prefer...  11.5 us
    dot_general x1, matrix products, on_device(): jnp.dot(basis.T, hidden_slab, precision=lax.Precision.HIGHEST, preferred_...  11.3 us
  transfers between devices with their start and end apart: 3, of which 3 were waited for; matrix products, arithmetic and copies ran while one was open for 1% of the time, Pallas kernels for 0%

commit v1 on v0

v1 whole, which is shorter than its diff:
```python
import functools

import jax
import jax.numpy as jnp
from jax import lax
from jax.experimental import pallas as pl
from jax.experimental.pallas import tpu as pltpu
from jax.sharding import PartitionSpec as P

F32 = jnp.float32
BF16 = jnp.bfloat16
HIGHEST = lax.Precision.HIGHEST
MESH = pl.DeviceIdType.MESH

NZ = 8
NP = 32
K = 288
HALF = K // 2
CH = 256
W = 1024
BLK = 32

NN = (((1,), (0,)), ((), ()))
NT = (((1,), (1,)), ((), ()))
TN = (((0,), (0,)), ((), ()))

PIECES = [(i, t) for i in range(K // 16) for t in range((16 * i + 15) // 128 + 1)]


def split(x):
    hi = x.astype(BF16)
    return hi, (x - hi.astype(F32)).astype(BF16)


def mm(a, b, dims=NN):
    return lax.dot_general(a, b, dims, preferred_element_type=F32)


def inv_chol(d):
    nt = BLK // 8
    lane = lax.broadcasted_iota(jnp.int32, (8, 128), 1)
    sub = lax.broadcasted_iota(jnp.int32, (8, 128), 0)
    n = [
        jnp.where(lane < BLK, d[8 * t : 8 * t + 8], jnp.where(lane == BLK + 8 * t + sub, 1.0, 0.0))
        for t in range(nt)
    ]
    for t in range(nt):
        c = [None] * nt
        for s in range(t, nt):
            c[s] = [jnp.broadcast_to(n[s][:, 8 * t + k : 8 * t + k + 1], (8, 128)) for k in range(8)]
        pv = jnp.ones((8, 128), F32)
        for j in range(8):
            p = jnp.broadcast_to(c[t][j][j : j + 1], (8, 128))
            pv = jnp.where(sub == j, p, pv)
            r = 1.0 / p
            f = [None] * nt
            for s in range(t, nt):
                f[s] = c[s][j] * r
                if s == t:
                    f[s] = jnp.where(sub > j, f[s], 0.0)
            for k in range(j + 1, 8):
                row = jnp.broadcast_to(c[t][k][j : j + 1], (8, 128))
                for s in range(t, nt):
                    c[s][k] = c[s][k] - f[s] * row
            row = jnp.broadcast_to(n[t][j : j + 1], (8, 128))
            for s in range(t, nt):
                n[s] = n[s] - f[s] * row
        n[t] = n[t] * lax.rsqrt(pv)
    return jnp.concatenate(n, axis=0)


def chol_step(m, k):
    lo = k * BLK
    row = m[lo : lo + BLK, :]
    lane = lax.broadcasted_iota(jnp.int32, row.shape, 1)
    sub = lax.broadcasted_iota(jnp.int32, row.shape, 0)
    d = pltpu.roll(row, 384 - lo, 1)[:, :128] if lo else row[:, :128]
    li = inv_chol(d)[:, BLK : 2 * BLK]
    row = jnp.where((lane >= lo) & (lane < lo + BLK), jnp.where(lane - lo == sub, 1.0, 0.0), row)
    r = jnp.dot(li, row, precision=HIGHEST, preferred_element_type=F32)
    m[lo : lo + BLK, :] = r
    if lo + BLK < K:
        upd = lax.dot_general(
            r[:, lo + BLK : K], r, TN, precision=HIGHEST, preferred_element_type=F32
        )
        rest = m[lo + BLK : K, :]
        lane = lax.broadcasted_iota(jnp.int32, rest.shape, 1)
        m[lo + BLK : K, :] = jnp.where((lane >= lo) & (lane < lo + BLK), 0.0, rest) - upd


def kernel(
    scale,
    slab_hbm,
    test_hbm,
    basis_hbm,
    proj_ref,
    slab,
    test,
    slab_hi,
    slab_lo,
    tst,
    part,
    rbuf,
    sg,
    wacc,
    gfull,
    gp,
    gr,
    gz,
    ga,
    m,
    lp,
    qs,
    qx,
    qr,
    bout,
    in_sem,
    rs_ss,
    rs_rs,
    ag_ss,
    ag_rs,
    g1_ss,
    g1_rs,
    g2_ss,
    g2_rs,
    g3_ss,
    g3_rs,
    cx_ss,
    cx_rs,
    q_ss,
    q_rs,
    out_sem,
):
    z = lax.axis_index("col")
    r = lax.axis_index("row")
    core = lax.rem(r, 2)
    chip = r // 2

    def zdev(j):
        return (r, lax.rem(z + j, NZ))

    def rdev(i):
        return (lax.rem(r + i, NP), z)

    def remote(src, dst, ss, rs, dev):
        return pltpu.make_async_remote_copy(
            src_ref=src, dst_ref=dst, send_sem=ss, recv_sem=rs, device_id=dev, device_id_type=MESH
        )

    def dest(k):
        near = lax.div(k + 1, 2)
        off = jnp.where(lax.rem(k, 2) == 1, 4 - near, 4 + near)
        return lax.rem(z + off, NZ)

    def slab_copy(k):
        rows = pl.ds(pl.multiple_of(dest(k) * CH, CH), CH)
        return pltpu.make_async_copy(slab_hbm.at[rows, :], slab.at[rows, :], in_sem.at[k])

    test_copy = pltpu.make_async_copy(test_hbm, test, in_sem.at[NZ])
    test_copy.start()

    @pl.loop(0, NZ)
    def _(k):
        slab_copy(k).start()

    barrier = pltpu.get_barrier_semaphore()

    @pl.loop(1, NP)
    def _(i):
        pl.semaphore_signal(barrier, inc=1, device_id=rdev(i), device_id_type=MESH)

    @pl.loop(1, NZ)
    def _(j):
        pl.semaphore_signal(barrier, inc=1, device_id=zdev(j), device_id_type=MESH)

    test_copy.wait()
    tt = test[...].T
    th, tl = split(tt)
    tst[0:K, :] = th
    tst[K : 2 * K, :] = tl

    def half(direction, i):
        return pl.ds(HALF * ((i + direction) % 2), HALF)

    def rs_copy(direction, i):
        step = (i + 1) // 2
        off = 4 - step if direction == 0 else 4 + step
        src = part.at[lax.rem(z + off, NZ), half(direction, i)]
        dev = zdev(1 if direction == 0 else NZ - 1)
        return remote(src, rbuf.at[direction, i], rs_ss.at[direction, i], rs_rs.at[direction, i], dev)

    @pl.loop(0, NZ)
    def _(k):
        d = dest(k)
        rows = pl.ds(pl.multiple_of(d * CH, CH), CH)
        slab_copy(k).wait()
        sh, sl = split(slab[rows, :])
        slab_hi[rows, :] = sh
        slab_lo[rows, :] = sl
        both = mm(tst[...], sh, NT)
        part[d] = both[:K] + both[K:] + mm(tst[0:K, :], sl, NT)

        @pl.when(k == 0)
        def _():
            pl.semaphore_wait(barrier, NP - 1 + NZ - 1)
            rs_copy(0, 0).start()
            rs_copy(1, 0).start()

        @pl.when(k == 1)
        def _():
            rs_copy(0, 1).start()

        @pl.when(k == 2)
        def _():
            rs_copy(1, 1).start()

    for i in range(5):
        for direction in range(2):
            rs_copy(direction, i).wait_recv()
            step = (i + 3) // 2
            off = 4 - step if direction == 0 else 4 + step
            d = lax.rem(z + off, NZ)
            h = half(direction, i)
            part[d, h, :] = part[d, h, :] + rbuf[direction, i]
            rs_copy(direction, i + 2).start()
    for i in (5, 6):
        for direction in range(2):
            rs_copy(direction, i).wait_recv()
    for lo, up, down in ((0, 6, 5), (1, 5, 6)):
        h = pl.ds(HALF * lo, HALF)
        sg[z, h, :] = part[z, h, :] + (rbuf[0, up] + rbuf[1, down])

    def ag_copy(direction, i):
        c = lax.rem(z + NZ - i // 2, NZ) if direction == 0 else lax.rem(z + i // 2, NZ)
        ref = sg.at[c, half(direction, i)]
        dev = zdev(1 if direction == 0 else NZ - 1)
        return remote(ref, ref, ag_ss.at[direction, i], ag_rs.at[direction, i], dev)

    def ag_recv(direction, i):
        c = lax.rem(z + NZ - 1 - i // 2, NZ) if direction == 0 else lax.rem(z + 1 + i // 2, NZ)
        ref = sg.at[c, half(direction, i)]
        dev = zdev(1 if direction == 0 else NZ - 1)
        return remote(ref, ref, ag_ss.at[direction, i], ag_rs.at[direction, i], dev)

    def ag_forward(i):
        for direction in range(2):
            ag_recv(direction, i).wait_recv()
            if i < 5:
                ag_copy(direction, i + 2).start()

    for i in range(2):
        for direction in range(2):
            ag_copy(direction, i).start()

    own = sg[z]
    gfull[:, 256:384] = jnp.zeros((K, 128), F32)
    gfull[:, 0:K] = lax.dot_general(own, own, NT, precision=HIGHEST, preferred_element_type=F32)
    gp[len(PIECES) : NP] = jnp.zeros((NP - len(PIECES), 16, 128), F32)
    for p, (i, t) in enumerate(PIECES):
        gp[p] = gfull[16 * i : 16 * i + 16, 128 * t : 128 * t + 128]
    gr[r] = gp[r]

    def g1_copy(i):
        return remote(gp.at[lax.rem(r + i, NP)], gr.at[r], g1_ss.at[i], g1_rs.at[i], rdev(i))

    def g2_copy(j):
        return remote(gz.at[z], gz.at[z], g2_ss.at[j], g2_rs.at[j], zdev(j))

    def g3_copy(i):
        return remote(ga.at[r], ga.at[r], g3_ss.at[i], g3_rs.at[i], rdev(i))

    @pl.loop(1, NP)
    def _(i):
        g1_copy(i).start()

    def w_add(c):
        rows = pl.ds(pl.multiple_of(c * CH, CH), CH)
        sh, sl = split(sg[c])
        both = jnp.concatenate([sh, sl], axis=0)

        @pl.loop(0, W // 256)
        def _(n):
            cols = pl.ds(pl.multiple_of(n * 256, 256), 256)
            xh = slab_hi[rows, cols]
            y = mm(both, xh)
            wacc[:, cols] = wacc[:, cols] + (y[:K] + y[K:] + mm(sh, slab_lo[rows, cols]))

    wacc[...] = jnp.zeros((K, W), F32)
    w_add(z)
    ag_forward(0)

    @pl.loop(1, NP)
    def _(i):
        g1_copy(i).wait_recv()

    gz[z] = jnp.sum(gr[...], axis=0)

    @pl.loop(1, NZ)
    def _(j):
        g2_copy(j).start()

    ag_forward(1)

    @pl.loop(0, 2)
    def _(n):
        w_add(lax.rem(z + jnp.where(n == 0, 1, NZ - 1), NZ))

    ag_forward(2)

    @pl.loop(1, NZ)
    def _(j):
        g2_copy(j).wait_recv()

    ga[r] = jnp.sum(gz[...], axis=0)

    @pl.loop(1, NP)
    def _(i):
        g3_copy(i).start()

    ag_forward(3)

    @pl.loop(0, 2)
    def _(n):
        w_add(lax.rem(z + jnp.where(n == 0, 2, NZ - 2), NZ))

    ag_forward(4)

    @pl.loop(1, NP)
    def _(i):
        g3_copy(i).wait_recv()

    for p, (i, t) in enumerate(PIECES):
        m[16 * i : 16 * i + 16, 128 * t : 128 * t + 128] = ga[p]
    m[0:128, 128:256] = m[128:256, 0:128].T
    m[0:256, 256:K] = m[256:K, 0:256].T

    for k in range(K // BLK):
        chol_step(m, k)
        if k == 2:
            ag_forward(5)
        if k == 4:
            ag_forward(6)

    @pl.loop(3, 6)
    def _(n):
        w_add(lax.rem(z + n, NZ))

    shape = (K, K)
    tri = lax.broadcasted_iota(jnp.int32, shape, 1) <= lax.broadcasted_iota(jnp.int32, shape, 0)
    m[:, 0:K] = jnp.where(tri, m[:, 0:K], 0.0)
    for i in range(NP):
        lp[8 * i : 8 * i + 8, :] = m[9 * i : 9 * i + 8, 0:K]
        lp[256 + i : 257 + i, :] = m[9 * i + 8 : 9 * i + 9, 0:K]
    lh, ll = split(lp[...])
    lboth = jnp.concatenate([lh, ll], axis=0)

    @pl.loop(0, W // 256)
    def _(n):
        cols = pl.ds(pl.multiple_of(n * 256, 256), 256)
        wh, wl = split(wacc[:, cols])
        y = mm(lboth, wh)
        q = y[:K] + y[K:] + mm(lh, wl)
        for s in range(2):
            t = 2 * n + s
            q128 = q[:, 128 * s : 128 * s + 128]
            for i in range(NP):
                qs[i % 2, i // 2, t] = q128[8 * i : 8 * i + 8]
            for i in range(NP):
                qs[i % 2, i // 2, 8, pl.ds(t, 1), :] = q128[256 + i : 257 + i]

    cx = remote(qs.at[1 - core], qx, cx_ss, cx_rs, (r + 1 - 2 * core, z))
    cx.start()

    u = (m[:, 0:K] * scale).T
    uh, ul = split(u)
    cx.wait_recv()
    qs[core] = qs[core] + qx[...]

    def q_copy(i):
        to = lax.rem(chip + i, NP // 2)
        return remote(
            qs.at[core, to], qr.at[chip], q_ss.at[i], q_rs.at[i], (2 * to + core, z)
        )

    @pl.loop(1, NP // 2)
    def _(i):
        q_copy(i).start()

    def out_copy(c):
        rows = pl.ds(pl.multiple_of(c * CH, CH), CH)
        return pltpu.make_async_copy(bout.at[c], basis_hbm.at[rows, :], out_sem.at[c])

    @pl.loop(0, NZ)
    def _(c):
        sh, sl = split(sg[c].T)
        bout[c] = mm(sh, uh) + (mm(sl, uh) + mm(sh, ul))
        out_copy(c).start()

    qr[chip] = qs[core, chip]

    @pl.loop(1, NP // 2)
    def _(i):
        q_copy(i).wait_recv()

    total = jnp.sum(qr[...], axis=0)
    for t in range(8):
        proj_ref[0:8, 128 * t : 128 * t + 128] = total[t]
        proj_ref[8:9, 128 * t : 128 * t + 128] = total[8, t : t + 1]

    for direction in range(2):
        for i in range(7):
            rs_copy(direction, i).wait_send()
            ag_copy(direction, i).wait_send()

    @pl.loop(1, NP)
    def _(i):
        g1_copy(i).wait_send()
        g3_copy(i).wait_send()

    @pl.loop(1, NZ)
    def _(j):
        g2_copy(j).wait_send()

    cx.wait_send()

    @pl.loop(1, NP // 2)
    def _(i):
        q_copy(i).wait_send()

    @pl.loop(0, NZ)
    def _(c):
        out_copy(c).wait()


def on_device(hidden_slab, test_matrix):
    rows, cols = hidden_slab.shape
    total_rows = rows * lax.axis_size("row")
    dma = pltpu.SemaphoreType.DMA
    return pl.pallas_call(
        functools.partial(kernel, float(total_rows) ** 0.5),
        out_shape=(
            jax.ShapeDtypeStruct((rows, K), F32),
            jax.ShapeDtypeStruct((K // NP, cols), F32),
        ),
        in_specs=[pl.BlockSpec(memory_space=pl.ANY)] * 2,
        out_specs=(pl.BlockSpec(memory_space=pl.ANY), pl.BlockSpec(memory_space=pltpu.VMEM)),
        scratch_shapes=[
            pltpu.VMEM((rows, cols), F32),
            pltpu.VMEM((cols, K), F32),
            pltpu.VMEM((rows, cols), BF16),
            pltpu.VMEM((rows, cols), BF16),
            pltpu.VMEM((2 * K, cols), BF16),
            pltpu.VMEM((NZ, K, CH), F32),
            pltpu.VMEM((2, 7, HALF, CH), F32),
            pltpu.VMEM((NZ, K, CH), F32),
            pltpu.VMEM((K, cols), F32),
            pltpu.VMEM((K, 384), F32),
            pltpu.VMEM((NP, 16, 128), F32),
            pltpu.VMEM((NP, 16, 128), F32),
            pltpu.VMEM((NZ, 16, 128), F32),
            pltpu.VMEM((NP, 16, 128), F32),
            pltpu.VMEM((K, 384), F32),
            pltpu.VMEM((K, K), F32),
            pltpu.VMEM((2, NP // 2, 9, 8, 128), F32),
            pltpu.VMEM((NP // 2, 9, 8, 128), F32),
            pltpu.VMEM((NP // 2, 9, 8, 128), F32),
            pltpu.VMEM((NZ, CH, K), F32),
            dma((NZ + 1,)),
            dma((2, 7)),
            dma((2, 7)),
            dma((2, 7)),
            dma((2, 7)),
            dma((NP,)),
            dma((NP,)),
            dma((NZ,)),
            dma((NZ,)),
            dma((NP,)),
            dma((NP,)),
            dma,
            dma,
            dma((NP // 2,)),
            dma((NP // 2,)),
            dma((NZ,)),
        ],
        compiler_params=pltpu.CompilerParams(
            collective_id=0, has_side_effects=True, vmem_limit_bytes=56 << 20
        ),
    )(hidden_slab, test_matrix)


def solution(mesh):
    return jax.shard_map(
        on_device,
        mesh=mesh,
        in_specs=(P("row", "col"), P("col", None)),
        out_specs=(P("row", None), P("row", "col")),
        check_vma=False,
    )
```

time: 488 us -> 96.8 us (0.20)
  waiting for transfers between devices: 308 us -> 0 us
  other arithmetic: 99.3 us -> 0 us
  Pallas kernels: 0 us -> 89.1 us
  matrix products: 44.8 us -> 0 us
  between operations: 16.5 us -> 0.65 us
  local copies, waits for them, and re-layouts: 18.3 us -> 6.89 us
    psum x2 -> x0, waiting for transfers between devices: 198 us -> none  [the longest x1 113 us: on_device(): gram = lax.psum(gram_local, 'row')]
    unnamed x4 -> x0, waiting for transfers between devices: 110 us -> none
    another operation x17 -> x0, other arithmetic: 95 us -> none  [the longest x10 59.4 us: on_device(): factor = jnp.linalg.cholesky(gram)]
    pallas_call x0 -> x1, Pallas kernels: none -> 89.1 us  [on_device(): pl.pallas_call(functools.partial(kernel, float(total_rows) ** 0.5), out_s...]
    dot_general x3 -> x0, matrix products: 29.7 us -> none  [the longest x1 11.5 us: on_device(): jnp.dot(hidden_slab, test_matrix, precision=lax.Precision.HIGHEST, prefer...]
    another operation x9 -> x0, matrix products: 15.1 us -> none  [the longest x5 8.93 us: on_device(): basis = jax.scipy.linalg.solve_triangular(factor, sketch.T, lower=True).T]
    another operation x11 -> x0, local copies, waits for them, and re-layouts: 12.3 us -> none
  transfers between devices with their start and end apart: 3 -> 0, of which waited for: 3 -> 0; matrix products, arithmetic and copies ran while one was open for 1% -> 0% of each run, Pallas kernels for 0% -> 0%
where the time goes in v1:
time: 96.8 us; the launch traced here: 96.7 us
  Pallas kernels  89.1 us (92%)
  local copies, waits for them, and re-layouts  6.89 us (7%)
    pallas_call x1, Pallas kernels, on_device(): pl.pallas_call(functools.partial(kernel, float(total_rows) ** 0.5), out_s...  89.1 us
    unnamed x4, local copies, waits for them, and re-layouts  3.52 us
    pallas_call x1, local copies, waits for them, and re-layouts, on_device(): pl.pallas_call(functools.partial(kernel, float(total_rows) ** 0.5), out_s...  3.38 us

profile of v1, /device:TPU:1, one launch (start us, length us, event | category | flops | bytes accessed | tf_op | source)
XLA Modules:
  0.0 96.7 jit_solution(2612879952997743294)
XLA Ops:
  0.6 2.9 %copy.4.test_hbm = f32[1024,288]{1,0:T(8,128)} copy(f32[1024,288]{0,1:T(8,128)} %param.3) | data formatting | bytes 2359296 | tf_op args[1]
  3.5 89.1 %shard_map.41 = (f32[2048,288]{1,0:T(8,128)}, f32[9,1024]{1,0:T(8,128)}) custom-call(f32[2048,1024]{1,0:T(8,128)} %slab_hbm.1, f32[1024,288]{1,0:T(8,128)} %copy.4.test_hbm), custom_call_target="tpu_custom_call" | custom-call | tf_op jit(solution)/shard_map/pallas_call | solution.py:439
  92.6 0.0 copy-start
  92.7 3.4 %copy.5 = f32[2048,288]{0,1:T(8,128)} copy(f32[2048,288]{1,0:T(8,128)} %get-tuple-element.2) | data formatting | bytes 4718592 | tf_op jit(solution)/shard_map/pallas_call | solution.py:439
  96.0 0.0 copy-done
  96.0 0.6 copy.7
Async XLA Ops:
  92.6 3.4 %copy-start = (f32[9,1024]{1,0:T(8,128)S(1)}, f32[9,1024]{1,0:T(8,128)}, u32[]{:S(2)}) copy-start(f32[9,1024]{1,0:T(8,128)} %get-tuple-element.7) | copy-start | bytes 110596

commit v2 on v1

--- a/solution.py
+++ b/solution.py
@@ -79,20 +79,19 @@
     row = jnp.where((lane >= lo) & (lane < lo + BLK), jnp.where(lane - lo == sub, 1.0, 0.0), row)
     r = jnp.dot(li, row, precision=HIGHEST, preferred_element_type=F32)
     m[lo : lo + BLK, :] = r
-    if lo + BLK < K:
-        upd = lax.dot_general(
-            r[:, lo + BLK : K], r, TN, precision=HIGHEST, preferred_element_type=F32
-        )
-        rest = m[lo + BLK : K, :]
-        lane = lax.broadcasted_iota(jnp.int32, rest.shape, 1)
-        m[lo + BLK : K, :] = jnp.where((lane >= lo) & (lane < lo + BLK), 0.0, rest) - upd
+    for a, b in ((lo + BLK, lo + 2 * BLK), (lo + 2 * BLK, K)):
+        if a < K:
+            upd = lax.dot_general(r[:, a:b], r, TN, precision=HIGHEST, preferred_element_type=F32)
+            rest = m[a:b, :]
+            lane = lax.broadcasted_iota(jnp.int32, rest.shape, 1)
+            m[a:b, :] = jnp.where((lane >= lo) & (lane < lo + BLK), 0.0, rest) - upd
 
 
 def kernel(
     scale,
     slab_hbm,
-    test_hbm,
-    basis_hbm,
+    test_t_hbm,
+    basis_t_ref,
     proj_ref,
     slab,
     test,
@@ -113,7 +112,6 @@
     qs,
     qx,
     qr,
-    bout,
     in_sem,
     rs_ss,
     rs_rs,
@@ -129,7 +127,6 @@
     cx_rs,
     q_ss,
     q_rs,
-    out_sem,
 ):
     z = lax.axis_index("col")
     r = lax.axis_index("row")
@@ -156,7 +153,7 @@
         rows = pl.ds(pl.multiple_of(dest(k) * CH, CH), CH)
         return pltpu.make_async_copy(slab_hbm.at[rows, :], slab.at[rows, :], in_sem.at[k])
 
-    test_copy = pltpu.make_async_copy(test_hbm, test, in_sem.at[NZ])
+    test_copy = pltpu.make_async_copy(test_t_hbm, test, in_sem.at[NZ])
     test_copy.start()
 
     @pl.loop(0, NZ)
@@ -174,8 +171,7 @@
         pl.semaphore_signal(barrier, inc=1, device_id=zdev(j), device_id_type=MESH)
 
     test_copy.wait()
-    tt = test[...].T
-    th, tl = split(tt)
+    th, tl = split(test[...])
     tst[0:K, :] = th
     tst[K : 2 * K, :] = tl
 
@@ -273,21 +269,15 @@
     def _(i):
         g1_copy(i).start()
 
-    def w_add(c):
+    def w_add(off, first=False):
+        c = lax.rem(z + off, NZ)
         rows = pl.ds(pl.multiple_of(c * CH, CH), CH)
         sh, sl = split(sg[c])
-        both = jnp.concatenate([sh, sl], axis=0)
-
-        @pl.loop(0, W // 256)
-        def _(n):
-            cols = pl.ds(pl.multiple_of(n * 256, 256), 256)
-            xh = slab_hi[rows, cols]
-            y = mm(both, xh)
-            wacc[:, cols] = wacc[:, cols] + (y[:K] + y[K:] + mm(sh, slab_lo[rows, cols]))
-
-    wacc[...] = jnp.zeros((K, W), F32)
-    w_add(z)
-    ag_forward(0)
+        y = mm(jnp.concatenate([sh, sl], axis=0), slab_hi[rows, :])
+        y = y[:K] + y[K:] + mm(sh, slab_lo[rows, :])
+        wacc[...] = y if first else wacc[...] + y
+
+    w_add(0, first=True)
 
     @pl.loop(1, NP)
     def _(i):
@@ -299,13 +289,10 @@
     def _(j):
         g2_copy(j).start()
 
+    ag_forward(0)
     ag_forward(1)
-
-    @pl.loop(0, 2)
-    def _(n):
-        w_add(lax.rem(z + jnp.where(n == 0, 1, NZ - 1), NZ))
-
-    ag_forward(2)
+    w_add(1)
+    w_add(NZ - 1)
 
     @pl.loop(1, NZ)
     def _(j):
@@ -317,13 +304,8 @@
     def _(i):
         g3_copy(i).start()
 
+    ag_forward(2)
     ag_forward(3)
-
-    @pl.loop(0, 2)
-    def _(n):
-        w_add(lax.rem(z + jnp.where(n == 0, 2, NZ - 2), NZ))
-
-    ag_forward(4)
 
     @pl.loop(1, NP)
     def _(i):
@@ -336,14 +318,20 @@
 
     for k in range(K // BLK):
         chol_step(m, k)
-        if k == 2:
+        if k == 0:
+            w_add(2)
+        if k == 1:
+            w_add(NZ - 2)
+            ag_forward(4)
+        if k == 4:
             ag_forward(5)
-        if k == 4:
+        if k == 5:
+            w_add(3)
+        if k == 6:
+            w_add(NZ - 3)
             ag_forward(6)
-
-    @pl.loop(3, 6)
-    def _(n):
-        w_add(lax.rem(z + n, NZ))
+        if k == 7:
+            w_add(4)
 
     shape = (K, K)
     tri = lax.broadcasted_iota(jnp.int32, shape, 1) <= lax.broadcasted_iota(jnp.int32, shape, 0)
@@ -354,25 +342,20 @@
     lh, ll = split(lp[...])
     lboth = jnp.concatenate([lh, ll], axis=0)
 
-    @pl.loop(0, W // 256)
-    def _(n):
-        cols = pl.ds(pl.multiple_of(n * 256, 256), 256)
-        wh, wl = split(wacc[:, cols])
-        y = mm(lboth, wh)
-        q = y[:K] + y[K:] + mm(lh, wl)
-        for s in range(2):
-            t = 2 * n + s
-            q128 = q[:, 128 * s : 128 * s + 128]
-            for i in range(NP):
-                qs[i % 2, i // 2, t] = q128[8 * i : 8 * i + 8]
-            for i in range(NP):
-                qs[i % 2, i // 2, 8, pl.ds(t, 1), :] = q128[256 + i : 257 + i]
+    wh, wl = split(wacc[...])
+    y = mm(lboth, wh)
+    q = y[:K] + y[K:] + mm(lh, wl)
+    for t in range(W // 128):
+        q128 = q[:, 128 * t : 128 * t + 128]
+        for i in range(NP):
+            qs[i % 2, i // 2, t] = q128[8 * i : 8 * i + 8]
+            qs[i % 2, i // 2, 8, t : t + 1] = q128[256 + i : 257 + i]
 
     cx = remote(qs.at[1 - core], qx, cx_ss, cx_rs, (r + 1 - 2 * core, z))
     cx.start()
 
-    u = (m[:, 0:K] * scale).T
-    uh, ul = split(u)
+    bh, bl = split(m[:, 0:K] * scale)
+    bboth = jnp.concatenate([bh, bl], axis=0)
     cx.wait_recv()
     qs[core] = qs[core] + qx[...]
 
@@ -386,15 +369,12 @@
     def _(i):
         q_copy(i).start()
 
-    def out_copy(c):
-        rows = pl.ds(pl.multiple_of(c * CH, CH), CH)
-        return pltpu.make_async_copy(bout.at[c], basis_hbm.at[rows, :], out_sem.at[c])
-
     @pl.loop(0, NZ)
     def _(c):
-        sh, sl = split(sg[c].T)
-        bout[c] = mm(sh, uh) + (mm(sl, uh) + mm(sh, ul))
-        out_copy(c).start()
+        sh, sl = split(sg[c])
+        y = mm(bboth, sh)
+        rows = pl.ds(pl.multiple_of(c * CH, CH), CH)
+        basis_t_ref[:, rows] = y[:K] + y[K:] + mm(bh, sl)
 
     qr[chip] = qs[core, chip]
 
@@ -427,26 +407,22 @@
     def _(i):
         q_copy(i).wait_send()
 
-    @pl.loop(0, NZ)
-    def _(c):
-        out_copy(c).wait()
-
 
 def on_device(hidden_slab, test_matrix):
     rows, cols = hidden_slab.shape
     total_rows = rows * lax.axis_size("row")
     dma = pltpu.SemaphoreType.DMA
-    return pl.pallas_call(
+    basis_t, projected = pl.pallas_call(
         functools.partial(kernel, float(total_rows) ** 0.5),
         out_shape=(
-            jax.ShapeDtypeStruct((rows, K), F32),
-            jax.ShapeDtypeStruct((K // NP, cols), F32),
+            pltpu.VMEM((K, rows), F32),
+            pltpu.VMEM((K // NP, cols), F32),
         ),
         in_specs=[pl.BlockSpec(memory_space=pl.ANY)] * 2,
-        out_specs=(pl.BlockSpec(memory_space=pl.ANY), pl.BlockSpec(memory_space=pltpu.VMEM)),
+        out_specs=(pl.BlockSpec(memory_space=pltpu.VMEM), pl.BlockSpec(memory_space=pltpu.VMEM)),
         scratch_shapes=[
             pltpu.VMEM((rows, cols), F32),
-            pltpu.VMEM((cols, K), F32),
+            pltpu.VMEM((K, cols), F32),
             pltpu.VMEM((rows, cols), BF16),
             pltpu.VMEM((rows, cols), BF16),
             pltpu.VMEM((2 * K, cols), BF16),
@@ -464,8 +440,7 @@
             pltpu.VMEM((2, NP // 2, 9, 8, 128), F32),
             pltpu.VMEM((NP // 2, 9, 8, 128), F32),
             pltpu.VMEM((NP // 2, 9, 8, 128), F32),
-            pltpu.VMEM((NZ, CH, K), F32),
-            dma((NZ + 1,)),
+                dma((NZ + 1,)),
             dma((2, 7)),
             dma((2, 7)),
             dma((2, 7)),
@@ -480,12 +455,12 @@
             dma,
             dma((NP // 2,)),
             dma((NP // 2,)),
-            dma((NZ,)),
         ],
         compiler_params=pltpu.CompilerParams(
             collective_id=0, has_side_effects=True, vmem_limit_bytes=56 << 20
         ),
-    )(hidden_slab, test_matrix)
+    )(hidden_slab, test_matrix.T)
+    return basis_t.T, projected
 
 
 def solution(mesh):

time: 96.8 us -> 84.1 us (0.87)
  Pallas kernels: 89.1 us -> 81.3 us
  local copies, waits for them, and re-layouts: 6.89 us -> 2.04 us
    pallas_call x1, Pallas kernels: 89.1 us -> 81.3 us  [on_device(): pl.pallas_call(functools.partial(kernel, float(total_rows) ** 0.5), out_s...]
    pallas_call x1 -> x0, local copies, waits for them, and re-layouts: 3.38 us -> none  [on_device(): pl.pallas_call(functools.partial(kernel, float(total_rows) ** 0.5), out_s...]
    unnamed x4 -> x2, local copies, waits for them, and re-layouts: 3.52 us -> 2.04 us
where the time goes in v2:
time: 84.1 us; the launch traced here: 84 us
  Pallas kernels  81.3 us (97%)
  local copies, waits for them, and re-layouts  2.04 us (2%)
    pallas_call x1, Pallas kernels, on_device(): pl.pallas_call(functools.partial(kernel, float(total_rows) ** 0.5), out_s...  81.3 us
    unnamed x2, local copies, waits for them, and re-layouts  2.04 us

profile of v2, /device:TPU:1, one launch (start us, length us, event | category | flops | bytes accessed | tf_op | source)
XLA Modules:
  0.0 84.0 jit_solution(6657697232270230442)
XLA Ops:
  0.6 81.3 %shard_map.41 = (f32[288,2048]{1,0:T(8,128)S(1)}, f32[9,1024]{1,0:T(8,128)S(1)}) custom-call(f32[2048,1024]{1,0:T(8,128)} %slab_hbm.1, f32[288,1024]{1,0:T(8,128)} %bitcast.3), custom_call_target="tpu_custom_call" | custom-call | tf_op jit(solution)/shard_map/pallas_call | solution.py:415
  81.9 1.4 %copy.6 = f32[2048,288]{0,1:T(8,128)} copy(f32[2048,288]{0,1:T(8,128)S(1)} %bitcast.2) | data formatting | bytes 4718592
  83.3 0.6 copy.7

commit v3 on v2

--- a/solution.py
+++ b/solution.py
@@ -18,7 +18,7 @@
 HALF = K // 2
 CH = 256
 W = 1024
-BLK = 32
+BLK = 48
 
 NN = (((1,), (0,)), ((), ()))
 NT = (((1,), (1,)), ((), ()))
@@ -156,9 +156,7 @@
     test_copy = pltpu.make_async_copy(test_t_hbm, test, in_sem.at[NZ])
     test_copy.start()
 
-    @pl.loop(0, NZ)
-    def _(k):
-        slab_copy(k).start()
+    slab_copy(0).start()
 
     barrier = pltpu.get_barrier_semaphore()
 
@@ -169,6 +167,10 @@
     @pl.loop(1, NZ)
     def _(j):
         pl.semaphore_signal(barrier, inc=1, device_id=zdev(j), device_id_type=MESH)
+
+    @pl.loop(1, NZ)
+    def _(k):
+        slab_copy(k).start()
 
     test_copy.wait()
     th, tl = split(test[...])
@@ -305,7 +307,6 @@
         g3_copy(i).start()
 
     ag_forward(2)
-    ag_forward(3)
 
     @pl.loop(1, NP)
     def _(i):
@@ -316,21 +317,22 @@
     m[0:128, 128:256] = m[128:256, 0:128].T
     m[0:256, 256:K] = m[256:K, 0:256].T
 
+    ag_forward(3)
     for k in range(K // BLK):
         chol_step(m, k)
         if k == 0:
             w_add(2)
+            ag_forward(4)
         if k == 1:
             w_add(NZ - 2)
-            ag_forward(4)
+        if k == 2:
+            ag_forward(5)
+        if k == 3:
+            w_add(3)
         if k == 4:
-            ag_forward(5)
-        if k == 5:
-            w_add(3)
-        if k == 6:
             w_add(NZ - 3)
             ag_forward(6)
-        if k == 7:
+        if k == 5:
             w_add(4)
 
     shape = (K, K)
@@ -342,33 +344,47 @@
     lh, ll = split(lp[...])
     lboth = jnp.concatenate([lh, ll], axis=0)
 
-    wh, wl = split(wacc[...])
-    y = mm(lboth, wh)
-    q = y[:K] + y[K:] + mm(lh, wl)
-    for t in range(W // 128):
-        q128 = q[:, 128 * t : 128 * t + 128]
-        for i in range(NP):
-            qs[i % 2, i // 2, t] = q128[8 * i : 8 * i + 8]
-            qs[i % 2, i // 2, 8, t : t + 1] = q128[256 + i : 257 + i]
-
-    cx = remote(qs.at[1 - core], qx, cx_ss, cx_rs, (r + 1 - 2 * core, z))
-    cx.start()
+    tiles = (pl.ds(0, 4), pl.ds(4, 5))
+
+    def cx_copy(h):
+        return remote(
+            qs.at[1 - core, :, tiles[h]],
+            qx.at[:, tiles[h]],
+            cx_ss.at[h],
+            cx_rs.at[h],
+            (r + 1 - 2 * core, z),
+        )
+
+    def q_copy(h, i):
+        to = lax.rem(chip + i, NP // 2)
+        return remote(
+            qs.at[core, to, tiles[h]],
+            qr.at[chip, tiles[h]],
+            q_ss.at[h, i],
+            q_rs.at[h, i],
+            (2 * to + core, z),
+        )
+
+    for h in range(2):
+        wh, wl = split(wacc[:, 512 * h : 512 * h + 512])
+        y = mm(lboth, wh)
+        q = y[:K] + y[K:] + mm(lh, wl)
+        for t in range(4 * h, 4 * h + 4):
+            q128 = q[:, 128 * (t - 4 * h) : 128 * (t - 4 * h) + 128]
+            for i in range(NP):
+                qs[i % 2, i // 2, t] = q128[8 * i : 8 * i + 8]
+                qs[i % 2, i // 2, 8, t : t + 1] = q128[256 + i : 257 + i]
+        cx_copy(h).start()
+    for h in range(2):
+        cx_copy(h).wait_recv()
+        qs[core, :, tiles[h]] = qs[core, :, tiles[h]] + qx[:, tiles[h]]
+
+        @pl.loop(1, NP // 2)
+        def _(i):
+            q_copy(h, i).start()
 
     bh, bl = split(m[:, 0:K] * scale)
     bboth = jnp.concatenate([bh, bl], axis=0)
-    cx.wait_recv()
-    qs[core] = qs[core] + qx[...]
-
-    def q_copy(i):
-        to = lax.rem(chip + i, NP // 2)
-        return remote(
-            qs.at[core, to], qr.at[chip], q_ss.at[i], q_rs.at[i], (2 * to + core, z)
-        )
-
-    @pl.loop(1, NP // 2)
-    def _(i):
-        q_copy(i).start()
-
     @pl.loop(0, NZ)
     def _(c):
         sh, sl = split(sg[c])
@@ -380,7 +396,8 @@
 
     @pl.loop(1, NP // 2)
     def _(i):
-        q_copy(i).wait_recv()
+        for h in range(2):
+            q_copy(h, i).wait_recv()
 
     total = jnp.sum(qr[...], axis=0)
     for t in range(8):
@@ -401,11 +418,13 @@
     def _(j):
         g2_copy(j).wait_send()
 
-    cx.wait_send()
+    for h in range(2):
+        cx_copy(h).wait_send()
 
     @pl.loop(1, NP // 2)
     def _(i):
-        q_copy(i).wait_send()
+        for h in range(2):
+            q_copy(h, i).wait_send()
 
 
 def on_device(hidden_slab, test_matrix):
@@ -451,10 +470,10 @@
             dma((NZ,)),
             dma((NP,)),
             dma((NP,)),
-            dma,
-            dma,
-            dma((NP // 2,)),
-            dma((NP // 2,)),
+            dma((2,)),
+            dma((2,)),
+            dma((2, NP // 2)),
+            dma((2, NP // 2)),
         ],
         compiler_params=pltpu.CompilerParams(
             collective_id=0, has_side_effects=True, vmem_limit_bytes=56 << 20

time: 84.1 us -> 82.5 us (0.981)
  Pallas kernels: 81.3 us -> 79.7 us
    pallas_call x1, Pallas kernels: 81.3 us -> 79.7 us  [on_device(): pl.pallas_call(functools.partial(kernel, float(total_rows) ** 0.5), out_s...]
where the time goes in v3:
time: 82.5 us; the launch traced here: 82.4 us
  Pallas kernels  79.7 us (97%)
  local copies, waits for them, and re-layouts  2.04 us (2%)
    pallas_call x1, Pallas kernels, on_device(): pl.pallas_call(functools.partial(kernel, float(total_rows) ** 0.5), out_s...  79.7 us
    unnamed x2, local copies, waits for them, and re-layouts  2.04 us

profile of v3, /device:TPU:1, one launch (start us, length us, event | category | flops | bytes accessed | tf_op | source)
XLA Modules:
  0.0 82.4 jit_solution(5720620577923284939)
XLA Ops:
  0.6 79.7 %shard_map.41 = (f32[288,2048]{1,0:T(8,128)S(1)}, f32[9,1024]{1,0:T(8,128)S(1)}) custom-call(f32[2048,1024]{1,0:T(8,128)} %slab_hbm.1, f32[288,1024]{1,0:T(8,128)} %bitcast.3), custom_call_target="tpu_custom_call" | custom-call | tf_op jit(solution)/shard_map/pallas_call | solution.py:434
  80.4 1.4 %copy.6 = f32[2048,288]{0,1:T(8,128)} copy(f32[2048,288]{0,1:T(8,128)S(1)} %bitcast.2) | data formatting | bytes 4718592
  81.8 0.6 copy.7

commit v4 on v3

--- a/solution.py
+++ b/solution.py
@@ -271,13 +271,14 @@
     def _(i):
         g1_copy(i).start()
 
-    def w_add(off, first=False):
+    def w_add(off, h=None, first=False):
         c = lax.rem(z + off, NZ)
         rows = pl.ds(pl.multiple_of(c * CH, CH), CH)
-        sh, sl = split(sg[c])
+        lo, n = (0, K) if h is None else (HALF * h, HALF)
+        sh, sl = split(sg[c, lo : lo + n, :])
         y = mm(jnp.concatenate([sh, sl], axis=0), slab_hi[rows, :])
-        y = y[:K] + y[K:] + mm(sh, slab_lo[rows, :])
-        wacc[...] = y if first else wacc[...] + y
+        y = y[:n] + y[n:] + mm(sh, slab_lo[rows, :])
+        wacc[lo : lo + n, :] = y if first else wacc[lo : lo + n, :] + y
 
     w_add(0, first=True)
 
@@ -307,6 +308,8 @@
         g3_copy(i).start()
 
     ag_forward(2)
+    w_add(NZ - 2, 0)
+    w_add(2, 1)
 
     @pl.loop(1, NP)
     def _(i):
@@ -317,114 +320,126 @@
     m[0:128, 128:256] = m[128:256, 0:128].T
     m[0:256, 256:K] = m[256:K, 0:256].T
 
+    def chips(h):
+        return pl.ds(NP // 4 * h, NP // 4)
+
+    def cx_copy(h):
+        return remote(
+            qs.at[1 - core, chips(h)], qx.at[chips(h)], cx_ss.at[h], cx_rs.at[h], (r + 1 - 2 * core, z)
+        )
+
+    def q_copy(to):
+        return remote(
+            qs.at[core, to], qr.at[chip], q_ss.at[to], q_rs.at[chip], (2 * to + core, z)
+        )
+
+    def q_recv(s):
+        return remote(qs.at[core, s], qr.at[s], q_ss.at[s], q_rs.at[s], (2 * s + core, z))
+
+    def project(h):
+        lo, hi = HALF * h, HALF * (h + 1)
+        col = lax.broadcasted_iota(jnp.int32, (HALF, hi), 1)
+        row = lax.broadcasted_iota(jnp.int32, (HALF, hi), 0) + lo
+        m[lo:hi, 0:hi] = jnp.where(col <= row, m[lo:hi, 0:hi], 0.0)
+        for i in range(NP // 2):
+            lp[8 * i : 8 * i + 8, 0:hi] = m[lo + 9 * i : lo + 9 * i + 8, 0:hi]
+            lp[128 + i : 129 + i, 0:hi] = m[lo + 9 * i + 8 : lo + 9 * i + 9, 0:hi]
+        lh, ll = split(lp[:, 0:hi])
+        wh, wl = split(wacc[0:hi, :])
+        y = mm(jnp.concatenate([lh, ll], axis=0), wh)
+        q = y[:HALF] + y[HALF:] + mm(lh, wl)
+        for t in range(W // 128):
+            q128 = q[:, 128 * t : 128 * t + 128]
+            for i in range(NP // 2):
+                to = NP // 4 * h + i // 2
+                qs[i % 2, to, t] = q128[8 * i : 8 * i + 8]
+                qs[i % 2, to, 8, t : t + 1] = q128[128 + i : 129 + i]
+        cx_copy(h).start()
+
+    def scatter(h):
+        cx_copy(h).wait_recv()
+        qs[core, chips(h)] = qs[core, chips(h)] + qx[chips(h)]
+
+        @pl.loop(0, NP // 4)
+        def _(i):
+            to = NP // 4 * h + lax.rem(chip + i, NP // 4)
+
+            @pl.when(to != chip)
+            def _():
+                q_copy(to).start()
+
     ag_forward(3)
     for k in range(K // BLK):
         chol_step(m, k)
         if k == 0:
-            w_add(2)
+            w_add(NZ - 2, 1)
+            w_add(2, 0)
             ag_forward(4)
         if k == 1:
-            w_add(NZ - 2)
+            w_add(NZ - 3, 0)
+            w_add(3, 1)
         if k == 2:
             ag_forward(5)
         if k == 3:
-            w_add(3)
+            w_add(NZ - 3, 1)
+            w_add(3, 0)
+            ag_forward(6)
         if k == 4:
-            w_add(NZ - 3)
-            ag_forward(6)
-        if k == 5:
             w_add(4)
+            project(0)
+    scatter(0)
+    project(1)
 
     shape = (K, K)
     tri = lax.broadcasted_iota(jnp.int32, shape, 1) <= lax.broadcasted_iota(jnp.int32, shape, 0)
-    m[:, 0:K] = jnp.where(tri, m[:, 0:K], 0.0)
-    for i in range(NP):
-        lp[8 * i : 8 * i + 8, :] = m[9 * i : 9 * i + 8, 0:K]
-        lp[256 + i : 257 + i, :] = m[9 * i + 8 : 9 * i + 9, 0:K]
-    lh, ll = split(lp[...])
-    lboth = jnp.concatenate([lh, ll], axis=0)
-
-    tiles = (pl.ds(0, 4), pl.ds(4, 5))
-
-    def cx_copy(h):
-        return remote(
-            qs.at[1 - core, :, tiles[h]],
-            qx.at[:, tiles[h]],
-            cx_ss.at[h],
-            cx_rs.at[h],
-            (r + 1 - 2 * core, z),
-        )
-
-    def q_copy(h, i):
-        to = lax.rem(chip + i, NP // 2)
-        return remote(
-            qs.at[core, to, tiles[h]],
-            qr.at[chip, tiles[h]],
-            q_ss.at[h, i],
-            q_rs.at[h, i],
-            (2 * to + core, z),
-        )
-
-    for h in range(2):
-        wh, wl = split(wacc[:, 512 * h : 512 * h + 512])
-        y = mm(lboth, wh)
-        q = y[:K] + y[K:] + mm(lh, wl)
-        for t in range(4 * h, 4 * h + 4):
-            q128 = q[:, 128 * (t - 4 * h) : 128 * (t - 4 * h) + 128]
-            for i in range(NP):
-                qs[i % 2, i // 2, t] = q128[8 * i : 8 * i + 8]
-                qs[i % 2, i // 2, 8, t : t + 1] = q128[256 + i : 257 + i]
-        cx_copy(h).start()
-    for h in range(2):
-        cx_copy(h).wait_recv()
-        qs[core, :, tiles[h]] = qs[core, :, tiles[h]] + qx[:, tiles[h]]
-
-        @pl.loop(1, NP // 2)
-        def _(i):
-            q_copy(h, i).start()
-
-    bh, bl = split(m[:, 0:K] * scale)
+    bh, bl = split(jnp.where(tri, m[:, 0:K] * scale, 0.0))
     bboth = jnp.concatenate([bh, bl], axis=0)
-    @pl.loop(0, NZ)
-    def _(c):
+
+    def basis(c):
         sh, sl = split(sg[c])
         y = mm(bboth, sh)
         rows = pl.ds(pl.multiple_of(c * CH, CH), CH)
         basis_t_ref[:, rows] = y[:K] + y[K:] + mm(bh, sl)
 
+    basis(0)
+    scatter(1)
+    pl.loop(1, NZ)(basis)
+
+    for direction in range(2):
+        for i in range(7):
+            rs_copy(direction, i).wait_send()
+            ag_copy(direction, i).wait_send()
+
+    @pl.loop(1, NP)
+    def _(i):
+        g1_copy(i).wait_send()
+        g3_copy(i).wait_send()
+
+    @pl.loop(1, NZ)
+    def _(j):
+        g2_copy(j).wait_send()
+
+    for h in range(2):
+        cx_copy(h).wait_send()
+
+    @pl.loop(0, NP // 2)
+    def _(to):
+        @pl.when(to != chip)
+        def _():
+            q_copy(to).wait_send()
+
     qr[chip] = qs[core, chip]
 
-    @pl.loop(1, NP // 2)
-    def _(i):
-        for h in range(2):
-            q_copy(h, i).wait_recv()
+    @pl.loop(0, NP // 2)
+    def _(s):
+        @pl.when(s != chip)
+        def _():
+            q_recv(s).wait_recv()
 
     total = jnp.sum(qr[...], axis=0)
     for t in range(8):
         proj_ref[0:8, 128 * t : 128 * t + 128] = total[t]
         proj_ref[8:9, 128 * t : 128 * t + 128] = total[8, t : t + 1]
-
-    for direction in range(2):
-        for i in range(7):
-            rs_copy(direction, i).wait_send()
-            ag_copy(direction, i).wait_send()
-
-    @pl.loop(1, NP)
-    def _(i):
-        g1_copy(i).wait_send()
-        g3_copy(i).wait_send()
-
-    @pl.loop(1, NZ)
-    def _(j):
-        g2_copy(j).wait_send()
-
-    for h in range(2):
-        cx_copy(h).wait_send()
-
-    @pl.loop(1, NP // 2)
-    def _(i):
-        for h in range(2):
-            q_copy(h, i).wait_send()
 
 
 def on_device(hidden_slab, test_matrix):
@@ -455,7 +470,7 @@
             pltpu.VMEM((NZ, 16, 128), F32),
             pltpu.VMEM((NP, 16, 128), F32),
             pltpu.VMEM((K, 384), F32),
-            pltpu.VMEM((K, K), F32),
+            pltpu.VMEM((HALF, K), F32),
             pltpu.VMEM((2, NP // 2, 9, 8, 128), F32),
             pltpu.VMEM((NP // 2, 9, 8, 128), F32),
             pltpu.VMEM((NP // 2, 9, 8, 128), F32),
@@ -472,8 +487,8 @@
             dma((NP,)),
             dma((2,)),
             dma((2,)),
-            dma((2, NP // 2)),
-            dma((2, NP // 2)),
+            dma((NP // 2,)),
+            dma((NP // 2,)),
         ],
         compiler_params=pltpu.CompilerParams(
             collective_id=0, has_side_effects=True, vmem_limit_bytes=56 << 20

time: 82.5 us -> 80 us (0.970); the launches traced: 82.4 us -> 78.9 us
  Pallas kernels: 79.7 us -> 76.2 us
    pallas_call x1, Pallas kernels: 79.7 us -> 76.2 us  [on_device(): pl.pallas_call(functools.partial(kernel, float(total_rows) ** 0.5), out_s...]
where the time goes in v4:
time: 80 us; the launch traced here: 78.9 us
  Pallas kernels  76.2 us (95%)
  local copies, waits for them, and re-layouts  2.04 us (3%)
    pallas_call x1, Pallas kernels, on_device(): pl.pallas_call(functools.partial(kernel, float(total_rows) ** 0.5), out_s...  76.2 us
    unnamed x2, local copies, waits for them, and re-layouts  2.04 us

profile of v4, /device:TPU:1, one launch (start us, length us, event | category | flops | bytes accessed | tf_op | source)
XLA Modules:
  0.0 78.9 jit_solution(1902353409539439065)
XLA Ops:
  0.6 76.2 %shard_map.41 = (f32[288,2048]{1,0:T(8,128)S(1)}, f32[9,1024]{1,0:T(8,128)S(1)}) custom-call(f32[2048,1024]{1,0:T(8,128)} %slab_hbm.1, f32[288,1024]{1,0:T(8,128)} %bitcast.3), custom_call_target="tpu_custom_call" | custom-call | tf_op jit(solution)/shard_map/pallas_call | solution.py:449
  76.8 1.4 %copy.6 = f32[2048,288]{0,1:T(8,128)} copy(f32[2048,288]{0,1:T(8,128)S(1)} %bitcast.2) | data formatting | bytes 4718592
  78.2 0.6 copy.7

commit v5 on v4

--- a/solution.py
+++ b/solution.py
@@ -187,8 +187,7 @@
         dev = zdev(1 if direction == 0 else NZ - 1)
         return remote(src, rbuf.at[direction, i], rs_ss.at[direction, i], rs_rs.at[direction, i], dev)
 
-    @pl.loop(0, NZ)
-    def _(k):
+    def sketch_chunk(k):
         d = dest(k)
         rows = pl.ds(pl.multiple_of(d * CH, CH), CH)
         slab_copy(k).wait()
@@ -197,6 +196,10 @@
         slab_lo[rows, :] = sl
         both = mm(tst[...], sh, NT)
         part[d] = both[:K] + both[K:] + mm(tst[0:K, :], sl, NT)
+
+    @pl.loop(0, NZ - 1)
+    def _(k):
+        sketch_chunk(k)
 
         @pl.when(k == 0)
         def _():
@@ -221,6 +224,8 @@
             h = half(direction, i)
             part[d, h, :] = part[d, h, :] + rbuf[direction, i]
             rs_copy(direction, i + 2).start()
+        if i == 0:
+            sketch_chunk(jnp.int32(NZ - 1))
     for i in (5, 6):
         for direction in range(2):
             rs_copy(direction, i).wait_recv()

time: 80 us -> 80.5 us (level)
  no operation moved by 1% of the time
where the time goes in v5:
time: 80.5 us; the launch traced here: 79.3 us
  Pallas kernels  76.7 us (95%)
  local copies, waits for them, and re-layouts  2.04 us (3%)
    pallas_call x1, Pallas kernels, on_device(): pl.pallas_call(functools.partial(kernel, float(total_rows) ** 0.5), out_s...  76.7 us
    unnamed x2, local copies, waits for them, and re-layouts  2.04 us

profile of v5, /device:TPU:1, one launch (start us, length us, event | category | flops | bytes accessed | tf_op | source)
XLA Modules:
  0.0 79.3 jit_solution(15466316098116685210)
XLA Ops:
  0.6 76.7 %shard_map.41 = (f32[288,2048]{1,0:T(8,128)S(1)}, f32[9,1024]{1,0:T(8,128)S(1)}) custom-call(f32[2048,1024]{1,0:T(8,128)} %slab_hbm.1, f32[288,1024]{1,0:T(8,128)} %bitcast.3), custom_call_target="tpu_custom_call" | custom-call | tf_op jit(solution)/shard_map/pallas_call | solution.py:454
  77.3 1.4 %copy.6 = f32[2048,288]{0,1:T(8,128)} copy(f32[2048,288]{0,1:T(8,128)S(1)} %bitcast.2) | data formatting | bytes 4718592
  78.7 0.6 copy.7
